TPU v7x, 32 devices: a whole 2x2x4 slice. The times are simulated.
32 devices in a mesh: samp: 4 (over y, x), pre: 8 (over z, core).
Axes of the slice: x: 2, y: 2, z: 4, core: 2. Of those that a mesh axis runs over, the one named last changes fastest.
Arguments:
- queries: bfloat16 [64, 32, 128], P(('samp', 'pre')), may hold values from -15 to 15
- prefix_keys: bfloat16 [4, 6144, 128], P(None, ('pre', 'samp')), may hold values from -6 to 6
- prefix_values: bfloat16 [4, 6144, 128], P(None, ('pre', 'samp')), may hold values from -6 to 6
- suffix_keys: bfloat16 [64, 4, 128, 128], P(('samp', 'pre')), may hold values from -8 to 8
- suffix_values: bfloat16 [64, 4, 128, 128], P(('samp', 'pre')), may hold values from -6 to 6
- suffix_lengths: int32 [64], P(('samp', 'pre')), may hold values from 2 to 128, as said below
- prompt_length: int32 [1], replicated, may hold values from 3072 to 6144
- out_weight: bfloat16 [4096, 5120], P('pre'), may hold values from -0.09375 to 0.09375
Outputs:
- mixed: bfloat16 [64, 5120], P(('samp', 'pre'))
Inputs may be any that keep to these rules, and one draw needn't show every extreme that they name: `suffix_lengths`: some sample fills all 128 slots.
All inputs are finite; a program needn't handle non-finite values.
Results may differ from a plain program's by a relative error of at most 0.013.
Values may be sent and summed in bfloat16 or wider, within the bound.
A program may use at most 64 MiB of HBM per device.

v0:
```python
import math

import jax
import jax.numpy as jnp
from jax import lax
from jax.sharding import PartitionSpec as P

NEGATIVE = -1e30


def prompt_partial(grouped, block_keys, block_values, visible):
    scaling = 1.0 / math.sqrt(grouped.shape[-1])
    by_head = jnp.transpose(grouped, (1, 0, 2, 3))

    def one_head(operands):
        head_queries, head_keys, head_values = operands
        scores = (
            lax.dot_general(
                head_queries,
                head_keys,
                (((2,), (1,)), ((), ())),
                preferred_element_type=jnp.float32,
            )
            * scaling
        )
        scores = jnp.where(visible, scores, NEGATIVE)
        peaks = jnp.max(scores, axis=-1)
        weights = jnp.where(visible, jnp.exp(scores - peaks[..., None]), 0.0)
        totals = jnp.sum(weights, axis=-1)
        results = lax.dot_general(
            weights.astype(jnp.bfloat16),
            head_values,
            (((2,), (0,)), ((), ())),
            preferred_element_type=jnp.float32,
        )
        return (results.astype(jnp.bfloat16), peaks, totals)

    results, peaks, totals = lax.map(one_head, (by_head, block_keys, block_values))
    count = grouped.shape[0]
    heads = grouped.shape[1] * grouped.shape[2]
    results = jnp.transpose(results, (1, 0, 2, 3)).reshape(count, heads, grouped.shape[3])
    peaks = jnp.transpose(peaks, (1, 0, 2)).reshape(count, heads)
    totals = jnp.transpose(totals, (1, 0, 2)).reshape(count, heads)
    return (results, peaks, totals)


def suffix_partial(grouped, suffix_keys, suffix_values, suffix_lengths):
    scaling = 1.0 / math.sqrt(grouped.shape[-1])
    slots = suffix_keys.shape[2]
    visible = (jnp.arange(slots, dtype=jnp.int32)[None, :] < suffix_lengths[:, None])[
        :, None, None, :
    ]
    scores = (
        jnp.einsum("sgjd,sgpd->sgjp", grouped, suffix_keys, preferred_element_type=jnp.float32)
        * scaling
    )
    scores = jnp.where(visible, scores, NEGATIVE)
    peaks = jnp.max(scores, axis=-1)
    weights = jnp.where(visible, jnp.exp(scores - peaks[..., None]), 0.0)
    totals = jnp.sum(weights, axis=-1)
    results = jnp.einsum(
        "sgjp,sgpd->sgjd",
        weights.astype(jnp.bfloat16),
        suffix_values,
        preferred_element_type=jnp.float32,
    )
    count = grouped.shape[0]
    heads = grouped.shape[1] * grouped.shape[2]
    return (
        results.astype(jnp.bfloat16).reshape(count, heads, grouped.shape[3]),
        peaks.reshape(count, heads),
        totals.reshape(count, heads),
    )


def merge_parts(results, peaks, totals):
    highest = jnp.max(peaks, axis=0)
    weights = jnp.exp(peaks - highest)
    denominator = jnp.sum(weights * totals, axis=0)
    numerator = jnp.sum(weights[..., None] * results.astype(jnp.float32), axis=0)
    return (numerator / denominator[..., None]).astype(jnp.bfloat16)


def shards(
    queries,
    prefix_keys,
    prefix_values,
    suffix_keys,
    suffix_values,
    suffix_lengths,
    prompt_length,
    out_weight,
):
    own_samples = queries.shape[0]
    heads = queries.shape[1]
    head_width = queries.shape[2]
    key_heads = prefix_keys.shape[0]
    ratio = heads // key_heads
    groups = lax.axis_size("pre")
    head_share = heads // groups
    block_keys, block_values = (
        lax.all_gather(prefix_keys, "samp", axis=1, tiled=True),
        lax.all_gather(prefix_values, "samp", axis=1, tiled=True),
    )
    block_length = block_keys.shape[1]
    group_queries = lax.all_gather(queries, "pre", axis=0, tiled=True)
    group_count = group_queries.shape[0]
    positions = lax.axis_index("pre") * block_length + jnp.arange(block_length, dtype=jnp.int32)
    visible = positions < prompt_length[0]
    own_grouped = queries.reshape(own_samples, key_heads, ratio, head_width)
    suffix_results, suffix_peaks, suffix_totals = suffix_partial(
        own_grouped, suffix_keys, suffix_values, suffix_lengths
    )
    group_grouped = group_queries.reshape(group_count, key_heads, ratio, head_width)
    prompt_results, prompt_peaks, prompt_totals = prompt_partial(
        group_grouped, block_keys, block_values, visible
    )
    received_results = lax.all_to_all(
        prompt_results[None], "pre", split_axis=1, concat_axis=0, tiled=True
    )
    received_peaks, received_totals = (
        lax.all_to_all(prompt_peaks[None], "pre", split_axis=1, concat_axis=0, tiled=True),
        lax.all_to_all(prompt_totals[None], "pre", split_axis=1, concat_axis=0, tiled=True),
    )
    attention = merge_parts(
        jnp.concatenate([received_results, suffix_results[None]], 0),
        jnp.concatenate([received_peaks, suffix_peaks[None]], 0),
        jnp.concatenate([received_totals, suffix_totals[None]], 0),
    )
    head_rows = lax.all_to_all(attention, "pre", split_axis=1, concat_axis=0, tiled=True)
    flat_rows = head_rows.reshape(group_count, head_share * head_width)
    return lax.psum_scatter(
        jnp.dot(flat_rows, out_weight, preferred_element_type=jnp.float32).astype(jnp.bfloat16),
        "pre",
        scatter_dimension=0,
        tiled=True,
    )


def solution(mesh):
    return jax.shard_map(
        shards,
        mesh=mesh,
        in_specs=(
            P(("samp", "pre"), None, None),
            P(None, ("pre", "samp"), None),
            P(None, ("pre", "samp"), None),
            P(("samp", "pre"), None, None, None),
            P(("samp", "pre"), None, None, None),
            P(("samp", "pre")),
            P(),
            P("pre", None),
        ),
        out_specs=P(("samp", "pre"), None),
        check_vma=False,
    )
```

profile of v0, /device:TPU:0, one launch (start us, length us, event | category | flops | bytes accessed | tf_op | source)
XLA Modules:
  0.0 155.6 jit_solution(9852784574958552540)
XLA Ops:
  6.5 16.0 %all_gather.9 = bf16[16,32,128]{2,1,0:T(8,128)(2,1)S(1)} all-gather(bf16[2,32,128]{2,1,0:T(8,128)(2,1)} %param.10), channel_id=1, replica_groups=mesh['samp'=4,'pre'=8] {'pre'}, dimensions={0}, use_global_device_ids=true | all-gather | bytes 147456 | tf_op jit(solution)/shard_map/all_gather | solution.py:106
  22.6 13.6 %all_gather.10 = bf16[4,768,128]{2,1,0:T(8,128)(2,1)S(1)} all-gather(bf16[4,192,128]{2,1,0:T(8,128)(2,1)} %param.11), channel_id=1, replica_groups=mesh['samp'=4,'pre'=8] {'samp'}, dimensions={1}, use_global_device_ids=true | all-gather | bytes 983040 | tf_op jit(solution)/shard_map/all_gather | solution.py:102
  36.1 10.6 %all_gather.11 = bf16[4,768,128]{2,1,0:T(8,128)(2,1)S(1)} all-gather(bf16[4,192,128]{2,1,0:T(8,128)(2,1)} %param.12), channel_id=1, replica_groups=mesh['samp'=4,'pre'=8] {'samp'}, dimensions={1}, use_global_device_ids=true | all-gather | bytes 983040 | tf_op jit(solution)/shard_map/all_gather | solution.py:103
  46.8 8.9 %while.15 = (s32[]{:T(128)}, bf16[4,16,8,128]{3,2,0,1:T(8,128)(2,1)}, f32[4,16,8]{1,2,0:T(8,128)S(1)}, f32[4,16,8]{1,2,0:T(8,128)S(1)}, bf16[4,16,8,128]{3,2,0,1...) while((s32[]{:T(128)}, ...), condition=%wide.region_3.4_spmd.clone, body=%wide.region_0.3_spmd.clone.sunk | while | flops 51234048 | bytes 1672313 | solution.py:38
  46.8 0.7 add_compare_fusion.2
  48.0 0.9 fusion.48
  49.0 0.7 add_compare_fusion.2
  50.2 0.9 fusion.48
  51.2 0.7 add_compare_fusion.2
  52.4 0.9 fusion.48
  53.4 0.7 add_compare_fusion.2
  54.7 0.9 fusion.48
  55.6 0.7 copy.37
  56.3 4.6 %all-to-all-start = ((f32[1,16,32]{2,0,1:T(1,128)}), f32[1,16,32]{2,0,1:T(1,128)S(1)}, u32[]{:S(2)}, u32[]{:S(2)}) async-start(f32[1,16,32]{2,0,1:T(1,128)} %copy.37), calls=%async_computation | async-start | bytes 16384 | tf_op jit(solution)/shard_map/all_to_all | solution.py:122
  61.3 0.7 copy.40
  62.0 4.5 %all-to-all-done = f32[1,16,32]{2,0,1:T(1,128)S(1)} async-done(((f32[1,16,32]{2,0,1:T(1,128)}), f32[1,16,32]{2,0,1:T(1,128)S(1)}, u32[]{:S(2)}, u32[]{:S(2)}) %all-to-all-start) | async-done | bytes 2080 | tf_op jit(solution)/shard_map/all_to_all | solution.py:122
  66.5 3.3 %all-to-all-start.2 = ((f32[1,16,32]{2,0,1:T(1,128)}), f32[1,16,32]{2,0,1:T(1,128)S(1)}, u32[]{:S(2)}, u32[]{:S(2)}) async-start(f32[1,16,32]{2,0,1:T(1,128)} %copy.40), calls=%async_computation.2 | async-start | bytes 16384 | tf_op jit(solution)/shard_map/all_to_all | solution.py:123
  70.1 5.3 %all-to-all-done.2 = f32[1,16,32]{2,0,1:T(1,128)S(1)} async-done(((f32[1,16,32]{2,0,1:T(1,128)}), f32[1,16,32]{2,0,1:T(1,128)S(1)}, u32[]{:S(2)}, u32[]{:S(2)}) %all-to-all-start.2) | async-done | bytes 2080 | tf_op jit(solution)/shard_map/all_to_all | solution.py:123
  75.4 3.4 %all-to-all-start.1 = ((bf16[1,16,32,128]{3,2,0,1:T(8,128)(2,1)}), bf16[1,16,32,128]{3,2,0,1:T(8,128)(2,1)S(1)}, u32[]{:S(2)}, u32[]{:S(2)}) async-start(bf16[1,16,32,128]{3,2,0,1:T(8,128)(2,1)} %bitcast.9), calls=%async_computation.1 | async-start | bytes 262144 | tf_op jit(solution)/shard_map/all_to_all | solution.py:118
  79.3 6.2 %all-to-all-done.1 = bf16[1,16,32,128]{3,2,0,1:T(8,128)(2,1)S(1)} async-done(((bf16[1,16,32,128]{3,2,0,1:T(8,128)(2,1)}), bf16[1,16,32,128]{3,2,0,1:T(8,128)(2,1)S(1)}, u32[]{:S(2)}, u32[]{:S(2)}) %all-to-all-start.1) | async-done | bytes 131104 | tf_op jit(solution)/shard_map/all_to_all | solution.py:118
  85.7 8.1 %all_to_all.48 = bf16[2,32,128]{2,0,1:T(2,128)(2,1)S(1)} all-to-all(bf16[2,32,128]{2,0,1:T(2,128)(2,1)S(1)} %copy.41), channel_id=1, replica_groups=mesh['samp'=4,'pre'=8] {'pre'}, dimensions={1} | all-to-all | bytes 32768 | tf_op jit(solution)/shard_map/all_to_all | solution.py:130
  93.8 3.9 %convolution_convert_fusion.1 = bf16[16,5120]{1,0:T(8,128)(2,1)} fusion(bf16[512,5120]{1,0:T(8,128)(2,1)} %param.17, bf16[2,8,4,128]{3,2,1,0:T(4,128)(2,1)S(1)} %bitcast.78), kind=kOutput, calls=%fused_computation.24 | convolution fusion | flops 83968000 | bytes 5423104 | tf_op jit(solution)/shard_map/dot_general | solution.py:133
  99.1 48.2 %all-reduce.3.cloned.1.call-done = bf16[16,5120]{1,0:T(8,128)(2,1)} async-done(((bf16[16,5120]{1,0:T(8,128)(2,1)}), bf16[16,5120]{1,0:T(8,128)(2,1)}) %all-reduce.3.cloned.1.call-update) | async-done | bytes 163856
  147.3 1.5 constant_dynamic-slice_fusion
  (51 shorter events, 4.6 us)
Async XLA Ops:
  6.5 54.4 %copy-start = (bf16[2,4,128,128]{3,2,1,0:T(8,128)(2,1)S(1)}, bf16[2,4,128,128]{3,2,1,0:T(8,128)(2,1)}, u32[]{:S(2)}) copy-start(bf16[2,4,128,128]{3,2,1,0:T(8,128)(2,1)} %param.13) | copy-start | bytes 786436
  22.6 38.3 %copy-start.3 = (s32[2]{0:T(128)S(1)}, s32[2]{0:T(128)}, u32[]{:S(2)}) copy-start(s32[2]{0:T(128)} %param.15) | copy-start | bytes 28
  22.6 38.4 %copy-start.1 = (bf16[2,32,128]{2,1,0:T(8,128)(2,1)S(1)}, bf16[2,32,128]{2,1,0:T(8,128)(2,1)}, u32[]{:S(2)}) copy-start(bf16[2,32,128]{2,1,0:T(8,128)(2,1)} %param.10) | copy-start | bytes 49156
  36.1 33.7 %copy-start.2 = (bf16[2,4,128,128]{3,2,1,0:T(8,128)(2,1)S(1)}, bf16[2,4,128,128]{3,2,1,0:T(8,128)(2,1)}, u32[]{:S(2)}) copy-start(bf16[2,4,128,128]{3,2,1,0:T(8,128)(2,1)} %param.14) | copy-start | bytes 786436
  55.6 42.2 %copy-start.4 = (u32[32]{0:T(128)S(1)}, u32[32]{0:T(128)}, u32[]{:S(2)}) copy-start(u32[32]{0:T(128)} %constant.48) | copy-start | bytes 388
  56.3 10.2 %all-to-all-start = ((f32[1,16,32]{2,0,1:T(1,128)}), f32[1,16,32]{2,0,1:T(1,128)S(1)}, u32[]{:S(2)}, u32[]{:S(2)}) async-start(f32[1,16,32]{2,0,1:T(1,128)} %copy.37), calls=%async_computation | async-start | bytes 16384 | tf_op jit(solution)/shard_map/all_to_all | solution.py:122
  66.5 8.9 %all-to-all-start.2 = ((f32[1,16,32]{2,0,1:T(1,128)}), f32[1,16,32]{2,0,1:T(1,128)S(1)}, u32[]{:S(2)}, u32[]{:S(2)}) async-start(f32[1,16,32]{2,0,1:T(1,128)} %copy.40), calls=%async_computation.2 | async-start | bytes 16384 | tf_op jit(solution)/shard_map/all_to_all | solution.py:123
  75.4 10.1 %all-to-all-start.1 = ((bf16[1,16,32,128]{3,2,0,1:T(8,128)(2,1)}), bf16[1,16,32,128]{3,2,0,1:T(8,128)(2,1)S(1)}, u32[]{:S(2)}, u32[]{:S(2)}) async-start(bf16[1,16,32,128]{3,2,0,1:T(8,128)(2,1)} %bitcast.9), calls=%async_computation.1 | async-start | bytes 262144 | tf_op jit(solution)/shard_map/all_to_all | solution.py:118
  78.8 68.5 %all-reduce.3.cloned.1.call-start = ((), (), s32[]{:S(2)}) async-start(), calls=%async_computation.4 | async-start | bytes 327680
Sparse Core Ops, SparseCore 0:
  97.9 49.2 all-reduce.2
where the time goes:
time: 156 us
  waiting for transfers between devices  64.2 us (41%)
  blocking collectives  48.3 us (31%)
  between operations  14.1 us (9%)
  starting transfers between devices  11.3 us (7%)
  matrix products  9.26 us (6%)
  local copies, waits for them, and re-layouts  4.31 us (3%)
  other arithmetic  3.97 us (3%)
    unnamed x2, waiting for transfers between devices  48.2 us
    all_gather x1, blocking collectives, shards(): group_queries = lax.all_gather(queries, 'pre', axis=0, tiled=True)  16 us
    all_gather x1, blocking collectives, shards(): lax.all_gather(prefix_keys, 'samp', axis=1, tiled=True)  13.6 us
    all_gather x1, blocking collectives, shards(): lax.all_gather(prefix_values, 'samp', axis=1, tiled=True)  10.6 us
    all_to_all x1, blocking collectives, shards(): lax.all_to_all(attention, 'pre', split_axis=1, concat_axis=0, tiled=True)  8.11 us
    all_to_all x1, waiting for transfers between devices, shards(): lax.all_to_all(prompt_results[None], 'pre', split_axis=1, concat_axis=0,...  6.18 us
    all_to_all x1, waiting for transfers between devices, shards(): lax.all_to_all(prompt_totals[None], 'pre', split_axis=1, concat_axis=0, t...  5.29 us
    all_to_all x1, starting transfers between devices, shards(): lax.all_to_all(prompt_peaks[None], 'pre', split_axis=1, concat_axis=0, ti...  4.6 us
  transfers between devices with their start and end apart: 4, of which 4 were waited for; matrix products, arithmetic and copies ran while one was open for 2% of the time, Pallas kernels for 0%

commit v1 on v0

--- a/solution.py
+++ b/solution.py
@@ -1,8 +1,11 @@
+import functools
 import math
 
 import jax
 import jax.numpy as jnp
 from jax import lax
+from jax.experimental import pallas as pl
+from jax.experimental.pallas import tpu as pltpu
 from jax.sharding import PartitionSpec as P
 
 NEGATIVE = -1e30
@@ -137,9 +140,407 @@
     )
 
 
+MESH = pl.DeviceIdType.MESH
+LOG2E = 1.4426950408889634
+CUTS = 8
+
+
+def head_of(samp, pre, key_heads):
+    return lax.rem(samp + pre // 2 + 2 * lax.rem(pre, 2), key_heads)
+
+
+def fused_kernel(
+    samp,
+    pre,
+    length_ref,
+    prompt_ref,
+    q_ref,
+    pk_ref,
+    pv_ref,
+    sk_ref,
+    sv_ref,
+    w_ref,
+    out_ref,
+    qf,
+    qstage,
+    qbuf,
+    kvbuf,
+    sk,
+    sv,
+    w,
+    sufstage,
+    sufbuf,
+    ostage,
+    obuf,
+    sstage,
+    sbuf,
+    tscr,
+    attscr,
+    cut,
+    rstage,
+    rbuf,
+    q_send,
+    q_recv,
+    kv_send,
+    kv_recv,
+    local_sem,
+    suf_send,
+    suf_recv,
+    o_send,
+    o_recv,
+    s_send,
+    s_recv,
+    r_send,
+    r_recv,
+):
+    key_heads = pk_ref.shape[0]
+    width = q_ref.shape[2]
+    share = pk_ref.shape[1]
+    total = samp * pre
+    g = lax.axis_index("samp")
+    b = lax.axis_index("pre")
+    me = g * pre + b
+    head = head_of(g, b, key_heads)
+    scale = LOG2E / math.sqrt(width)
+
+    def go(source, target, send, recv, to_samp, to_pre):
+        pltpu.make_async_remote_copy(
+            src_ref=source,
+            dst_ref=target,
+            send_sem=send,
+            recv_sem=recv,
+            device_id=(to_samp, to_pre),
+            device_id_type=MESH,
+        ).start()
+
+    def drain(ref, sem):
+        pltpu.make_async_copy(ref, ref, sem).wait()
+
+    barrier = pltpu.get_barrier_semaphore()
+
+    @pl.loop(1, total)
+    def _(i):
+        t = lax.rem(me + i, total)
+        pl.semaphore_signal(
+            barrier, inc=1, device_id=(t // pre, lax.rem(t, pre)), device_id_type=MESH
+        )
+
+    pltpu.make_async_copy(sk_ref, sk, local_sem.at[0]).start()
+    pltpu.make_async_copy(sv_ref, sv, local_sem.at[1]).start()
+    pltpu.make_async_copy(pk_ref.at[head], kvbuf.at[g, 0], kv_recv.at[g]).start()
+    pltpu.make_async_copy(pv_ref.at[head], kvbuf.at[g, 1], kv_recv.at[g]).start()
+    pltpu.make_async_copy(w_ref, w, local_sem.at[2]).start()
+
+    wide = q_ref[...].astype(jnp.float32)
+    qf[...] = wide
+    for h in range(key_heads):
+        for c in range(2):
+            for s in range(2):
+                row = 16 * h + 8 * c + 4 * s
+                tscr[pl.ds(row, 4), :] = qf[s, pl.ds(8 * h + 4 * c, 4), :]
+    for h in range(key_heads):
+        qstage[h] = tscr[pl.ds(16 * h, 16), :].astype(jnp.bfloat16)
+
+    pltpu.make_async_copy(qstage.at[head], qbuf.at[me], q_recv).start()
+    pl.semaphore_wait(barrier, total - 1)
+
+    @pl.loop(1, total)
+    def _(i):
+        t = lax.rem(me + i, total)
+        to_samp, to_pre = t // pre, lax.rem(t, pre)
+        go(
+            qstage.at[head_of(to_samp, to_pre, key_heads)],
+            qbuf.at[me],
+            q_send,
+            q_recv,
+            to_samp,
+            to_pre,
+        )
+
+    for step in range(1, samp):
+        to = lax.rem(g + step, samp)
+        his = head_of(to, b, key_heads)
+        go(pk_ref.at[his], kvbuf.at[g, 0], kv_send, kv_recv.at[g], to, b)
+        go(pv_ref.at[his], kvbuf.at[g, 1], kv_send, kv_recv.at[g], to, b)
+
+    pltpu.make_async_copy(sk_ref, sk, local_sem.at[0]).wait()
+    pltpu.make_async_copy(sv_ref, sv, local_sem.at[1]).wait()
+    slots = sk.shape[2]
+    rows = lax.broadcasted_iota(jnp.int32, (16, 2 * slots), 0)
+    cols = lax.broadcasted_iota(jnp.int32, (16, 2 * slots), 1)
+    second_row = lax.rem(rows, 8) >= 4
+    first_end = jnp.where(second_row, 0, length_ref[0])
+    second_end = jnp.where(second_row, length_ref[1], 0) + slots
+    seen = cols < jnp.where(cols < slots, first_end, second_end)
+    for h in range(key_heads):
+        keys = jnp.concatenate([sk[0, h], sk[1, h]], axis=0)
+        values = jnp.concatenate([sv[0, h], sv[1, h]], axis=0)
+        scores = lax.dot_general(
+            qstage[h], keys, (((1,), (1,)), ((), ())), preferred_element_type=jnp.float32
+        )
+        scores = jnp.where(seen, scores * scale, NEGATIVE)
+        peaks = jnp.max(scores, axis=1, keepdims=True)
+        weights = jnp.exp2(scores - peaks)
+        totals = jnp.sum(weights, axis=1, keepdims=True)
+        results = jnp.dot(weights.astype(jnp.bfloat16), values, preferred_element_type=jnp.float32)
+        peaks = jnp.broadcast_to(peaks, (16, width))
+        totals = jnp.broadcast_to(totals, (16, width))
+        for c in range(2):
+            sufstage[2 * h + c, 0:8] = results[8 * c : 8 * c + 8]
+            sufstage[2 * h + c, 8:16] = peaks[8 * c : 8 * c + 8]
+            sufstage[2 * h + c, 16:24] = totals[8 * c : 8 * c + 8]
+
+    pltpu.make_async_copy(sufstage.at[b], sufbuf.at[b], suf_recv).start()
+
+    @pl.loop(1, pre)
+    def _(i):
+        to = lax.rem(b + i, pre)
+        go(sufstage.at[to], sufbuf.at[b], suf_send, suf_recv, g, to)
+
+    drain(qbuf, q_recv)
+    queries = qbuf[...].reshape(total * 16, width)
+    count = total * 16
+    peak = sums = result = None
+    for step in range(samp):
+        slot = lax.rem(g + step, samp)
+        drain(kvbuf.at[slot], kv_recv.at[slot])
+        scores = lax.dot_general(
+            kvbuf[slot, 0],
+            queries,
+            (((1,), (1,)), ((), ())),
+            preferred_element_type=jnp.float32,
+        )
+        first = (b * samp + slot) * share
+        place = first + lax.broadcasted_iota(jnp.int32, (share, count), 0)
+        scores = jnp.where(place < prompt_ref[0], scores * scale, NEGATIVE)
+        new_peak = jnp.max(scores, axis=0, keepdims=True)
+        if step:
+            new_peak = jnp.maximum(new_peak, peak)
+        weights = jnp.exp2(scores - new_peak)
+        new_sums = jnp.sum(weights, axis=0, keepdims=True)
+        new_result = lax.dot_general(
+            kvbuf[slot, 1],
+            weights.astype(jnp.bfloat16),
+            (((0,), (0,)), ((), ())),
+            preferred_element_type=jnp.float32,
+        )
+        if step:
+            keep = jnp.exp2(peak - new_peak)
+            new_sums = new_sums + keep * sums
+            new_result = new_result + keep * result
+        peak, sums, result = new_peak, new_sums, new_result
+
+    per = pre * 16
+    for t in range(samp):
+        block = result[:, per * t : per * (t + 1)].T.reshape(pre, 2, 8, width)
+        for c in range(2):
+            ostage[t, c] = block[:, c].reshape(pre * 8, width).astype(jnp.bfloat16)
+        tile = lax.broadcasted_iota(jnp.int32, (8, per), 0)
+        sstage[t] = jnp.where(
+            tile == 0, peak[:, per * t : per * (t + 1)], sums[:, per * t : per * (t + 1)]
+        )
+
+    slot8 = pl.ds(pl.multiple_of(b * 8, 8), 8)
+    for step in range(samp):
+        to = lax.rem(g + step, samp)
+        for c in range(2):
+            k = 2 * head + c
+
+            def here(to=to, c=c):
+                pltpu.make_async_copy(ostage.at[to, c], obuf.at[b], o_recv).start()
+                pltpu.make_async_copy(sstage.at[to], sbuf.at[slot8], s_recv).start()
+
+            def there(to=to, c=c, k=k):
+                go(ostage.at[to, c], obuf.at[b], o_send, o_recv, to, k)
+                go(sstage.at[to], sbuf.at[slot8], s_send, s_recv, to, k)
+
+            if step:
+                there()
+            else:
+                pl.when(k == b)(here)
+                pl.when(k != b)(there)
+
+    drain(sufbuf, suf_recv)
+    suffix = sufbuf[...]
+    suffix_result = suffix[:, 0:8].reshape(pre * 8, width)
+    suffix_peak = suffix[:, 8:16].reshape(pre * 8, width)
+    suffix_total = suffix[:, 16:24].reshape(pre * 8, width)
+    drain(sbuf, s_recv)
+    peaks = sbuf[pl.ds(0, pre, stride=8), :]
+    totals = sbuf[pl.ds(1, pre, stride=8), :]
+    top = jnp.max(peaks, axis=0, keepdims=True)
+    shares = jnp.exp2(peaks - top)
+    bottom = jnp.sum(shares * totals, axis=0, keepdims=True)
+    stacked = jnp.concatenate(
+        [
+            shares,
+            jnp.broadcast_to(top, (8, per)),
+            jnp.broadcast_to(bottom, (8, per)),
+            jnp.zeros((per - 16 - pre, per), jnp.float32),
+        ],
+        axis=0,
+    )
+    tscr[...] = stacked.T
+    turned = tscr[...].reshape(pre, 2, 8, per)
+    turned = jnp.where(lax.rem(b, 2) == 0, turned[:, 0], turned[:, 1]).reshape(pre * 8, per)
+    drain(obuf, o_recv)
+    prompt_result = jnp.zeros((pre * 8, width), jnp.float32)
+    for i in range(pre):
+        prompt_result += turned[:, i : i + 1] * obuf[i].astype(jnp.float32)
+    prompt_peak = turned[:, pre : pre + 1]
+    prompt_total = turned[:, pre + 8 : pre + 9]
+    highest = jnp.maximum(prompt_peak, suffix_peak)
+    old = jnp.exp2(prompt_peak - highest)
+    new = jnp.exp2(suffix_peak - highest)
+    attscr[...] = (old * prompt_result + new * suffix_result) / (
+        old * prompt_total + new * suffix_total
+    )
+    attention = jnp.concatenate(
+        [attscr[pl.ds(j, 2 * pre, stride=4), :] for j in range(4)], axis=1
+    ).astype(jnp.bfloat16)
+
+    pltpu.make_async_copy(w_ref, w, local_sem.at[2]).wait()
+    lanes = cut.shape[2]
+    piece = cut.shape[0] * lanes
+    for p in range(0, CUTS, 2):
+        part = jnp.dot(
+            attention,
+            w[:, p * piece : (p + 2) * piece],
+            preferred_element_type=jnp.float32,
+        )
+        for i in range(2):
+            for n in range(cut.shape[0]):
+                at = i * piece + n * lanes
+                cut[n, pl.ds(p + i, 2 * pre, stride=CUTS), :] = part[:, at : at + lanes]
+    for n in range(cut.shape[0]):
+        rows = cut[n].reshape(pre, 2 * CUTS, lanes)
+        rstage[:, :, n * lanes : (n + 1) * lanes] = rows.astype(jnp.bfloat16)
+
+    pltpu.make_async_copy(rstage.at[b], rbuf.at[b], r_recv).start()
+
+    @pl.loop(1, pre)
+    def _(i):
+        to = lax.rem(b + i, pre)
+        go(rstage.at[to], rbuf.at[b], r_send, r_recv, g, to)
+
+    drain(rbuf, r_recv)
+    out_ref[...] = jnp.sum(rbuf[...].astype(jnp.float32), axis=0).astype(jnp.bfloat16)
+
+    drain(qbuf.at[pl.ds(0, total - 1)], q_send)
+    drain(kvbuf.at[pl.ds(0, samp - 1)], kv_send)
+    drain(sufbuf.at[pl.ds(0, pre - 1)], suf_send)
+    drain(rbuf.at[pl.ds(0, pre - 1)], r_send)
+    mine = (2 * head == b) | (2 * head + 1 == b)
+
+    @pl.when(mine)
+    def _():
+        drain(obuf.at[pl.ds(0, pre - 1)], o_send)
+        drain(sbuf.at[pl.ds(0, 8 * (pre - 1))], s_send)
+
+    @pl.when(jnp.logical_not(mine))
+    def _():
+        drain(obuf, o_send)
+        drain(sbuf, s_send)
+
+
+def fused_shards(
+    samp,
+    pre,
+    queries,
+    prefix_keys,
+    prefix_values,
+    suffix_keys,
+    suffix_values,
+    suffix_lengths,
+    prompt_length,
+    out_weight,
+):
+    own, heads, width = queries.shape
+    key_heads, share, _ = prefix_keys.shape
+    features = out_weight.shape[1]
+    piece = features // CUTS
+    total = samp * pre
+    bf16, f32 = jnp.bfloat16, jnp.float32
+    dma = pltpu.SemaphoreType.DMA
+    vmem = pl.BlockSpec(memory_space=pltpu.VMEM)
+    smem = pl.BlockSpec(memory_space=pltpu.SMEM)
+    hbm = pl.BlockSpec(memory_space=pl.ANY)
+    out = pl.pallas_call(
+        functools.partial(fused_kernel, samp, pre),
+        out_shape=jax.ShapeDtypeStruct((own * CUTS, piece), bf16),
+        in_specs=[smem, smem, vmem, hbm, hbm, hbm, hbm, hbm],
+        out_specs=vmem,
+        scratch_shapes=[
+            pltpu.VMEM((own, heads, width), f32),
+            pltpu.VMEM((key_heads, 16, width), bf16),
+            pltpu.VMEM((total, 16, width), bf16),
+            pltpu.VMEM((samp, 2, share, width), bf16),
+            pltpu.VMEM(suffix_keys.shape, bf16),
+            pltpu.VMEM(suffix_values.shape, bf16),
+            pltpu.VMEM(out_weight.shape, bf16),
+            pltpu.VMEM((pre, 24, width), f32),
+            pltpu.VMEM((pre, 24, width), f32),
+            pltpu.VMEM((samp, 2, pre * 8, width), bf16),
+            pltpu.VMEM((pre, pre * 8, width), bf16),
+            pltpu.VMEM((samp, 8, pre * 16), f32),
+            pltpu.VMEM((pre * 8, pre * 16), f32),
+            pltpu.VMEM((pre * 16, width), f32),
+            pltpu.VMEM((pre * 8, width), f32),
+            pltpu.VMEM((piece // 128, own * pre * CUTS, 128), f32),
+            pltpu.VMEM((pre, own * CUTS, piece), bf16),
+            pltpu.VMEM((pre, own * CUTS, piece), bf16),
+            dma,
+            dma,
+            dma,
+            dma((samp,)),
+            dma((3,)),
+            dma,
+            dma,
+            dma,
+            dma,
+            dma,
+            dma,
+            dma,
+            dma,
+        ],
+        compiler_params=pltpu.CompilerParams(
+            collective_id=0, has_side_effects=True, vmem_limit_bytes=40 * 1024 * 1024
+        ),
+        cost_estimate=pl.CostEstimate(
+            flops=300_000_000, bytes_accessed=7_000_000, transcendentals=400_000
+        ),
+    )(
+        suffix_lengths,
+        prompt_length,
+        queries,
+        prefix_keys,
+        prefix_values,
+        suffix_keys,
+        suffix_values,
+        out_weight,
+    )
+    return out.reshape(own, features)
+
+
 def solution(mesh):
+    samp, pre = mesh.shape["samp"], mesh.shape["pre"]
+
+    def body(queries, prefix_keys, *rest):
+        own, heads, width = queries.shape
+        key_heads = prefix_keys.shape[0]
+        fits = (
+            samp == key_heads
+            and pre == 2 * key_heads
+            and heads == 8 * key_heads
+            and own == 2
+            and pre * 16 == width
+        )
+        if fits:
+            return fused_shards(samp, pre, queries, prefix_keys, *rest)
+        return shards(queries, prefix_keys, *rest)
+
     return jax.shard_map(
-        shards,
+        body,
         mesh=mesh,
         in_specs=(
             P(("samp", "pre"), None, None),

time: 156 us -> 38.5 us (0.25)
  waiting for transfers between devices: 64.2 us -> 0 us
  blocking collectives: 48.3 us -> 0 us
  Pallas kernels: 0 us -> 29.3 us
  between operations: 14.1 us -> 0.67 us
  starting transfers between devices: 11.3 us -> 0 us
  matrix products: 9.26 us -> 0 us
  other arithmetic: 3.97 us -> 0 us
  local copies, waits for them, and re-layouts: 4.31 us -> 8.22 us
    unnamed x2 -> x0, waiting for transfers between devices: 48.2 us -> none
    all_gather x3 -> x0, blocking collectives: 40.2 us -> none  [the longest x1 16 us: shards(): group_queries = lax.all_gather(queries, 'pre', axis=0, tiled=True)]
    pallas_call x0 -> x1, Pallas kernels: none -> 29.3 us  [fused_shards(): pl.pallas_call(functools.partial(fused_kernel, samp, pre), out_shape=jax....]
    all_to_all x3 -> x0, waiting for transfers between devices: 16 us -> none  [the longest x1 6.18 us: shards(): lax.all_to_all(prompt_results[None], 'pre', split_axis=1, concat_axis=0,...]
    all_to_all x3 -> x0, starting transfers between devices: 11.3 us -> none  [the longest x1 4.6 us: shards(): lax.all_to_all(prompt_peaks[None], 'pre', split_axis=1, concat_axis=0, ti...]
    dot_general x11 -> x0, matrix products: 9.26 us -> none  [the longest x1 3.94 us: shards(): jnp.dot(flat_rows, out_weight, preferred_element_type=jnp.float32)]
    all_to_all x1 -> x0, blocking collectives: 8.11 us -> none  [shards(): lax.all_to_all(attention, 'pre', split_axis=1, concat_axis=0, tiled=True)]
    unnamed x12 -> x14, local copies, waits for them, and re-layouts: 2.12 us -> 7.6 us
  transfers between devices with their start and end apart: 4 -> 0, of which waited for: 4 -> 0; matrix products, arithmetic and copies ran while one was open for 2% -> 0% of each run, Pallas kernels for 0% -> 0%
where the time goes in v1:
time: 38.5 us; the launch traced here: 38.2 us
  Pallas kernels  29.3 us (76%)
  local copies, waits for them, and re-layouts  8.22 us (21%)
  between operations  0.67 us (2%)
    pallas_call x1, Pallas kernels, fused_shards(): pl.pallas_call(functools.partial(fused_kernel, samp, pre), out_shape=jax....  29.3 us
    unnamed x14, local copies, waits for them, and re-layouts  7.6 us

profile of v1, /device:TPU:0, one launch (start us, length us, event | category | flops | bytes accessed | tf_op | source)
XLA Modules:
  0.0 38.2 jit_solution(11265027235731814428)
XLA Ops:
  0.7 0.0 copy-start
  0.7 2.5 %copy-done = bf16[512,5120]{1,0:T(8,128)(2,1)S(1)} copy-done((bf16[512,5120]{1,0:T(8,128)(2,1)S(1)}, bf16[512,5120]{1,0:T(8,128)(2,1)}, u32[]{:S(2)}) %copy-start) | copy-done | bytes 5242904
  3.1 0.0 copy-start.1
  3.1 0.9 %copy-done.1 = bf16[2,4,128,128]{3,2,1,0:T(8,128)(2,1)S(1)} copy-done((bf16[2,4,128,128]{3,2,1,0:T(8,128)(2,1)S(1)}, bf16[2,4,128,128]{3,2,1,0:T(8,128)(2,1)}, u32[]{:S(2)}) %copy-start.1) | copy-done | bytes 262168
  4.1 0.0 copy-start.2
  4.1 0.9 %copy-done.2 = bf16[2,4,128,128]{3,2,1,0:T(8,128)(2,1)S(1)} copy-done((bf16[2,4,128,128]{3,2,1,0:T(8,128)(2,1)S(1)}, bf16[2,4,128,128]{3,2,1,0:T(8,128)(2,1)}, u32[]{:S(2)}) %copy-start.2) | copy-done | bytes 262168
  5.0 0.0 copy-start.3
  5.0 0.9 %copy-done.3 = bf16[4,192,128]{2,1,0:T(8,128)(2,1)S(1)} copy-done((bf16[4,192,128]{2,1,0:T(8,128)(2,1)S(1)}, bf16[4,192,128]{2,1,0:T(8,128)(2,1)}, u32[]{:S(2)}) %copy-start.3) | copy-done | bytes 196632
  6.0 0.0 copy-start.4
  6.0 0.9 %copy-done.4 = bf16[4,192,128]{2,1,0:T(8,128)(2,1)S(1)} copy-done((bf16[4,192,128]{2,1,0:T(8,128)(2,1)S(1)}, bf16[4,192,128]{2,1,0:T(8,128)(2,1)}, u32[]{:S(2)}) %copy-start.4) | copy-done | bytes 196632
  6.9 0.0 copy-start.5
  6.9 0.7 %copy-done.5 = bf16[2,32,128]{2,1,0:T(8,128)(2,1)S(1)} copy-done((bf16[2,32,128]{2,1,0:T(8,128)(2,1)S(1)}, bf16[2,32,128]{2,1,0:T(8,128)(2,1)}, u32[]{:S(2)}) %copy-start.5) | copy-done | bytes 16408
  7.6 0.0 copy-start.6
  7.6 0.7 %copy-done.6 = s32[2]{0:T(128)S(1)} copy-done((s32[2]{0:T(128)S(1)}, s32[2]{0:T(128)}, u32[]{:S(2)}) %copy-start.6) | copy-done | bytes 32
  8.3 29.3 %shard_map.82 = bf16[16,640]{1,0:T(8,128)(2,1)S(1)} custom-call(s32[2]{0:T(128)S(1)} %copy-done.6, s32[1]{0:T(128)S(6)} %copy.9.prompt_ref, bf16[2,32,128]{2,1,0:T(8,128)(2,1)S(1)} %copy-done.5, bf16[4,192,128]{2,1,0:T(8,128)(2,1)S(1)} %copy-done.3, bf16[4,192,128]{2,1,0:T(8,128)(2,1)S(1)} %copy-done.4, bf16[2,4,128,128]{3,2,1,0:T(8,128)(2,1)S(1)} %copy-done.1, ...), custom_call_target="tpu_custom_call" | custom-call | flops 300000000 | bytes 7000000 | tf_op jit(solution)/shard_map/pallas_call | solution.py:468
  37.5 0.6 %reshape.3 = bf16[2,5120]{1,0:T(2,128)(2,1)} reshape(bf16[16,640]{1,0:T(8,128)(2,1)S(1)} %shard_map.82) | data formatting | bytes 40960 | tf_op jit(solution)/shard_map/reshape | solution.py:522
Async XLA Ops:
  0.7 2.5 %copy-start = (bf16[512,5120]{1,0:T(8,128)(2,1)S(1)}, bf16[512,5120]{1,0:T(8,128)(2,1)}, u32[]{:S(2)}) copy-start(bf16[512,5120]{1,0:T(8,128)(2,1)} %w_ref.1) | copy-start | bytes 15728644
  3.1 0.9 %copy-start.1 = (bf16[2,4,128,128]{3,2,1,0:T(8,128)(2,1)S(1)}, bf16[2,4,128,128]{3,2,1,0:T(8,128)(2,1)}, u32[]{:S(2)}) copy-start(bf16[2,4,128,128]{3,2,1,0:T(8,128)(2,1)} %sk_ref.1) | copy-start | bytes 786436
  4.1 0.9 %copy-start.2 = (bf16[2,4,128,128]{3,2,1,0:T(8,128)(2,1)S(1)}, bf16[2,4,128,128]{3,2,1,0:T(8,128)(2,1)}, u32[]{:S(2)}) copy-start(bf16[2,4,128,128]{3,2,1,0:T(8,128)(2,1)} %sv_ref.1) | copy-start | bytes 786436
  5.0 0.9 %copy-start.3 = (bf16[4,192,128]{2,1,0:T(8,128)(2,1)S(1)}, bf16[4,192,128]{2,1,0:T(8,128)(2,1)}, u32[]{:S(2)}) copy-start(bf16[4,192,128]{2,1,0:T(8,128)(2,1)} %pk_ref.1) | copy-start | bytes 589828
  6.0 0.9 %copy-start.4 = (bf16[4,192,128]{2,1,0:T(8,128)(2,1)S(1)}, bf16[4,192,128]{2,1,0:T(8,128)(2,1)}, u32[]{:S(2)}) copy-start(bf16[4,192,128]{2,1,0:T(8,128)(2,1)} %pv_ref.1) | copy-start | bytes 589828
  6.9 0.7 %copy-start.5 = (bf16[2,32,128]{2,1,0:T(8,128)(2,1)S(1)}, bf16[2,32,128]{2,1,0:T(8,128)(2,1)}, u32[]{:S(2)}) copy-start(bf16[2,32,128]{2,1,0:T(8,128)(2,1)} %q_ref.1) | copy-start | bytes 49156
  7.6 0.7 %copy-start.6 = (s32[2]{0:T(128)S(1)}, s32[2]{0:T(128)}, u32[]{:S(2)}) copy-start(s32[2]{0:T(128)} %length_ref.1) | copy-start | bytes 28

commit v2 on v1

--- a/solution.py
+++ b/solution.py
@@ -161,6 +161,7 @@
     sv_ref,
     w_ref,
     out_ref,
+    qin,
     qf,
     qstage,
     qbuf,
@@ -216,6 +217,7 @@
     def drain(ref, sem):
         pltpu.make_async_copy(ref, ref, sem).wait()
 
+    pltpu.make_async_copy(q_ref, qin, local_sem.at[3]).start()
     barrier = pltpu.get_barrier_semaphore()
 
     @pl.loop(1, total)
@@ -231,8 +233,8 @@
     pltpu.make_async_copy(pv_ref.at[head], kvbuf.at[g, 1], kv_recv.at[g]).start()
     pltpu.make_async_copy(w_ref, w, local_sem.at[2]).start()
 
-    wide = q_ref[...].astype(jnp.float32)
-    qf[...] = wide
+    pltpu.make_async_copy(q_ref, qin, local_sem.at[3]).wait()
+    qf[...] = qin[...].astype(jnp.float32)
     for h in range(key_heads):
         for c in range(2):
             for s in range(2):
@@ -464,14 +466,15 @@
     dma = pltpu.SemaphoreType.DMA
     vmem = pl.BlockSpec(memory_space=pltpu.VMEM)
     smem = pl.BlockSpec(memory_space=pltpu.SMEM)
-    hbm = pl.BlockSpec(memory_space=pl.ANY)
+    hbm = pl.BlockSpec(memory_space=pltpu.HBM)
     out = pl.pallas_call(
         functools.partial(fused_kernel, samp, pre),
         out_shape=jax.ShapeDtypeStruct((own * CUTS, piece), bf16),
-        in_specs=[smem, smem, vmem, hbm, hbm, hbm, hbm, hbm],
+        in_specs=[smem, smem, hbm, hbm, hbm, hbm, hbm, hbm],
         out_specs=vmem,
         scratch_shapes=[
-            pltpu.VMEM((own, heads, width), f32),
+            pltpu.VMEM(queries.shape, bf16),
+            pltpu.VMEM(queries.shape, f32),
             pltpu.VMEM((key_heads, 16, width), bf16),
             pltpu.VMEM((total, 16, width), bf16),
             pltpu.VMEM((samp, 2, share, width), bf16),
@@ -493,7 +496,7 @@
             dma,
             dma,
             dma((samp,)),
-            dma((3,)),
+            dma((4,)),
             dma,
             dma,
             dma,
@@ -504,7 +507,7 @@
             dma,
         ],
         compiler_params=pltpu.CompilerParams(
-            collective_id=0, has_side_effects=True, vmem_limit_bytes=40 * 1024 * 1024
+            collective_id=0, has_side_effects=True, vmem_limit_bytes=60 * 1024 * 1024
         ),
         cost_estimate=pl.CostEstimate(
             flops=300_000_000, bytes_accessed=7_000_000, transcendentals=400_000

time: 38.5 us -> 32.3 us (0.84)
  local copies, waits for them, and re-layouts: 8.22 us -> 1.35 us
  Pallas kernels: 29.3 us -> 30 us
    unnamed x14 -> x0, local copies, waits for them, and re-layouts: 7.6 us -> none
    pallas_call x1, Pallas kernels: 29.3 us -> 30 us  [fused_shards(): pl.pallas_call(functools.partial(fused_kernel, samp, pre), out_shape=jax....]
    reshape x1, local copies, waits for them, and re-layouts: 0.62 us -> 1.35 us  [fused_shards(): return out.reshape(own, features)]
where the time goes in v2:
time: 32.3 us; the launch traced here: 32 us
  Pallas kernels  30 us (93%)
  local copies, waits for them, and re-layouts  1.35 us (4%)
  between operations  0.66 us (2%)
    pallas_call x1, Pallas kernels, fused_shards(): pl.pallas_call(functools.partial(fused_kernel, samp, pre), out_shape=jax....  30 us
    reshape x1, local copies, waits for them, and re-layouts, fused_shards(): return out.reshape(own, features)  1.35 us

profile of v2, /device:TPU:0, one launch (start us, length us, event | category | flops | bytes accessed | tf_op | source)
XLA Modules:
  0.0 32.0 jit_solution(8465156209143542688)
XLA Ops:
  0.7 30.0 %shard_map.82 = bf16[16,640]{1,0:T(8,128)(2,1)} custom-call(s32[2]{0:T(128)} %length_ref.1, s32[1]{0:T(128)S(6)} %copy.9.prompt_ref, bf16[2,32,128]{2,1,0:T(8,128)(2,1)} %q_ref.1, bf16[4,192,128]{2,1,0:T(8,128)(2,1)} %pk_ref.1, bf16[4,192,128]{2,1,0:T(8,128)(2,1)} %pv_ref.1, bf16[2,4,128,128]{3,2,1,0:T(8,128)(2,1)} %sk_ref.1, ...), custom_call_target="tpu_custom_call" | custom-call | flops 300000000 | bytes 7000000 | tf_op jit(solution)/shard_map/pallas_call | solution.py:470
  30.7 1.3 %reshape.3 = bf16[2,5120]{1,0:T(2,128)(2,1)} reshape(bf16[16,640]{1,0:T(8,128)(2,1)} %shard_map.82) | data formatting | bytes 40960 | tf_op jit(solution)/shard_map/reshape | solution.py:525

commit v3 on v2

--- a/solution.py
+++ b/solution.py
@@ -146,7 +146,7 @@
 
 
 def head_of(samp, pre, key_heads):
-    return lax.rem(samp + pre // 2 + 2 * lax.rem(pre, 2), key_heads)
+    return lax.rem(samp + 3 * (pre // 2) + 2 * lax.rem(pre, 2), key_heads)
 
 
 def fused_kernel(

time: 32.3 us -> 31.2 us (0.966)
  Pallas kernels: 30 us -> 28.8 us
    pallas_call x1, Pallas kernels: 30 us -> 28.8 us  [fused_shards(): pl.pallas_call(functools.partial(fused_kernel, samp, pre), out_shape=jax....]
where the time goes in v3:
time: 31.2 us; the launch traced here: 30.8 us
  Pallas kernels  28.8 us (92%)
  local copies, waits for them, and re-layouts  1.35 us (4%)
  between operations  0.66 us (2%)
    pallas_call x1, Pallas kernels, fused_shards(): pl.pallas_call(functools.partial(fused_kernel, samp, pre), out_shape=jax....  28.8 us
    reshape x1, local copies, waits for them, and re-layouts, fused_shards(): return out.reshape(own, features)  1.35 us

profile of v3, /device:TPU:0, one launch (start us, length us, event | category | flops | bytes accessed | tf_op | source)
XLA Modules:
  0.0 30.8 jit_solution(9030947134661026208)
XLA Ops:
  0.7 28.8 %shard_map.82 = bf16[16,640]{1,0:T(8,128)(2,1)} custom-call(s32[2]{0:T(128)} %length_ref.1, s32[1]{0:T(128)S(6)} %copy.9.prompt_ref, bf16[2,32,128]{2,1,0:T(8,128)(2,1)} %q_ref.1, bf16[4,192,128]{2,1,0:T(8,128)(2,1)} %pk_ref.1, bf16[4,192,128]{2,1,0:T(8,128)(2,1)} %pv_ref.1, bf16[2,4,128,128]{3,2,1,0:T(8,128)(2,1)} %sk_ref.1, ...), custom_call_target="tpu_custom_call" | custom-call | flops 300000000 | bytes 7000000 | tf_op jit(solution)/shard_map/pallas_call | solution.py:470
  29.5 1.3 %reshape.3 = bf16[2,5120]{1,0:T(2,128)(2,1)} reshape(bf16[16,640]{1,0:T(8,128)(2,1)} %shard_map.82) | data formatting | bytes 40960 | tf_op jit(solution)/shard_map/reshape | solution.py:525

commit v4 on v3

--- a/solution.py
+++ b/solution.py
@@ -146,7 +146,7 @@
 
 
 def head_of(samp, pre, key_heads):
-    return lax.rem(samp + 3 * (pre // 2) + 2 * lax.rem(pre, 2), key_heads)
+    return lax.rem(samp // 2 + pre // 4 + lax.rem(pre, 2), 2) * 2 + lax.rem(lax.rem(samp, 2) + pre // 2, 2)
 
 
 def fused_kernel(
@@ -343,7 +343,7 @@
         )
 
     slot8 = pl.ds(pl.multiple_of(b * 8, 8), 8)
-    for step in range(samp):
+    for step in (*range(1, samp), 0):
         to = lax.rem(g + step, samp)
         for c in range(2):
             k = 2 * head + c

time: 31.2 us -> 30.5 us (0.978)
  Pallas kernels: 28.8 us -> 28.2 us
    pallas_call x1, Pallas kernels: 28.8 us -> 28.2 us  [fused_shards(): pl.pallas_call(functools.partial(fused_kernel, samp, pre), out_shape=jax....]
where the time goes in v4:
time: 30.5 us; the launch traced here: 30.2 us
  Pallas kernels  28.2 us (92%)
  local copies, waits for them, and re-layouts  1.35 us (4%)
  between operations  0.66 us (2%)
    pallas_call x1, Pallas kernels, fused_shards(): pl.pallas_call(functools.partial(fused_kernel, samp, pre), out_shape=jax....  28.2 us
    reshape x1, local copies, waits for them, and re-layouts, fused_shards(): return out.reshape(own, features)  1.35 us

profile of v4, /device:TPU:0, one launch (start us, length us, event | category | flops | bytes accessed | tf_op | source)
XLA Modules:
  0.0 30.2 jit_solution(10433645403661296829)
XLA Ops:
  0.7 28.2 %shard_map.82 = bf16[16,640]{1,0:T(8,128)(2,1)} custom-call(s32[2]{0:T(128)} %length_ref.1, s32[1]{0:T(128)S(6)} %copy.9.prompt_ref, bf16[2,32,128]{2,1,0:T(8,128)(2,1)} %q_ref.1, bf16[4,192,128]{2,1,0:T(8,128)(2,1)} %pk_ref.1, bf16[4,192,128]{2,1,0:T(8,128)(2,1)} %pv_ref.1, bf16[2,4,128,128]{3,2,1,0:T(8,128)(2,1)} %sk_ref.1, ...), custom_call_target="tpu_custom_call" | custom-call | flops 300000000 | bytes 7000000 | tf_op jit(solution)/shard_map/pallas_call | solution.py:470
  28.9 1.3 %reshape.3 = bf16[2,5120]{1,0:T(2,128)(2,1)} reshape(bf16[16,640]{1,0:T(8,128)(2,1)} %shard_map.82) | data formatting | bytes 40960 | tf_op jit(solution)/shard_map/reshape | solution.py:525
